TPU v7x, 128 devices: a whole 4x4x4 slice. The times are simulated.
128 devices in a mesh: req: 32 (over y, z, core), grp: 4 (over x).
Axes of the slice: x: 4, y: 4, z: 4, core: 2. Of those that a mesh axis runs over, the one named last changes fastest.
Arguments:
- residual_in: bfloat16 [2048, 2048], P('grp'), may hold values from -6 to 6
- mixer_in: bfloat16 [2048, 3, 2048], P('grp', None, 'req'), may hold values from -6 to 6
- forget_floor: float32 [2048], replicated, may hold values from 0.3 to 0.97
- conv_weight: float32 [4, 2048], P(None, 'req'), may hold values from -3 to 3
- conv_edges: bfloat16 [128, 3, 2048], P('grp', None, 'req'), may hold values from -6 to 6
- state_in: float32 [128, 2048, 128], P('grp', 'req'), may hold values from -6 to 6
- accepted: int32 [128], P('grp'), may hold values from 0 to 16
- home_slot: int32 [128], replicated, may hold values from 0 to 127, each once
- gain_mixer: float32 [2048], P('req'), may hold values from 0.1 to 1.9
- w_out: bfloat16 [2048, 2048], P('req'), may hold values from -0.25 to 0.25
- gain_mlp: float32 [2048], replicated, may hold values from 0.1 to 1.9
- w_gate: bfloat16 [2048, 5632], P(None, 'req'), may hold values from -0.125 to 0.125
- w_up: bfloat16 [2048, 5632], P(None, 'req'), may hold values from -0.125 to 0.125
- w_down: bfloat16 [5632, 2048], P('req'), may hold values from -0.15625 to 0.15625
- gain_next: float32 [2048], replicated, may hold values from 0.1 to 1.9
- w_next: bfloat16 [2048, 3, 2048], P(None, None, 'req'), may hold values from -0.125 to 0.125
Outputs:
- next_mixer: bfloat16 [2048, 3, 2048], P('grp', None, 'req')
- kept_state: float32 [128, 2048, 128], P('grp', 'req')
- kept_edges: bfloat16 [128, 3, 2048], P('grp', None, 'req')
Inputs may be any that keep to these rules, and one draw needn't show every extreme that they name: `home_slot`: every row of the kept outputs is the home of exactly one request.
All inputs are finite; a program needn't handle non-finite values.
Results may differ from a plain program's by a relative error of at most 0.029.
Values may be sent and summed in bfloat16 or wider, within the bound.
A program may use at most 64 MiB of HBM per device.

v0:
```python
import jax
import jax.numpy as jnp
from jax import lax
from jax.sharding import PartitionSpec as P

EPSILON = 1e-06


def partner_2(block, axis, apart):
    count = lax.axis_size(axis)
    route = []
    for low in range(count):
        high = low | 1 << apart
        if high != low and high < count:
            route += [(low, high), (high, low)]
    return lax.ppermute(block, axis, route)


def scaled_norm(values_in, gain_row):
    widened = values_in.astype(jnp.float32)
    factor = lax.rsqrt(jnp.mean(widened * widened, axis=1, keepdims=True) + EPSILON)
    return (widened * factor * gain_row).astype(jnp.bfloat16)


def per_device(
    residual_in,
    mixer_in,
    forget_floor,
    conv_weight,
    conv_edges,
    state_in,
    accepted,
    home_slot,
    gain_mixer,
    w_out,
    gain_mlp,
    w_gate,
    w_up,
    w_down,
    gain_next,
    w_next,
):
    token_rows = residual_in.shape[0]
    model_width = residual_in.shape[1]
    local_width = mixer_in.shape[2]
    requests = state_in.shape[0]
    key_width = state_in.shape[2]
    draft_steps = token_rows // requests
    tap_count = conv_weight.shape[0]
    member = lax.axis_index("req")
    own_halves = mixer_in[:, 0:2]
    partner = partner_2(own_halves, "req", 0)
    lower_half = member % 2 == 0
    key_side = jnp.where(
        lower_half,
        jnp.concatenate([own_halves, partner], axis=2),
        jnp.concatenate([partner, own_halves], axis=2),
    )
    head_count = local_width // local_width
    key_start = member * local_width // key_width * key_width
    forget_low = lax.dynamic_slice_in_dim(forget_floor, key_start, head_count * key_width, 0)
    query = jax.nn.silu(key_side[:, 0].astype(jnp.float32))
    forget = forget_low + (1.0 - forget_low) * jax.nn.sigmoid(key_side[:, 1].astype(jnp.float32))
    keyed = 1.0 - forget
    sequence = jnp.concatenate(
        [conv_edges, mixer_in[:, 2].reshape(requests, draft_steps, local_width)], axis=1
    )
    seq_float = sequence.astype(jnp.float32)
    conv_input = sum(
        (
            conv_weight[offset] * seq_float[:, offset : offset + draft_steps]
            for offset in range(tap_count)
        )
    )

    def by_step(array_in, inner_width):
        shaped = array_in.reshape(requests, draft_steps, head_count, inner_width)
        return jnp.moveaxis(shaped, 1, 0)

    step_inputs = (
        by_step(query, key_width),
        by_step(forget, key_width),
        by_step(keyed, key_width),
        by_step(conv_input, local_width),
    )
    head_scale = key_width ** (-0.5)

    def advance(carry, inputs_now):
        current, kept, counter = carry
        q_step, f_step, k_step, v_step = inputs_now
        current = f_step[:, :, None, :] * current + v_step[:, :, :, None] * k_step[:, :, None, :]
        output = jnp.sum(current * q_step[:, :, None, :], axis=3) * head_scale
        kept = jnp.where((counter + 1 == accepted)[:, None, None, None], current, kept)
        return ((current, kept, counter + 1), output)

    begin_state = state_in.reshape(requests, head_count, local_width, key_width)
    carry_out, outputs = lax.scan(advance, (begin_state, begin_state, jnp.int32(0)), step_inputs)
    kept_local = carry_out[1].reshape(requests, local_width, key_width)
    mixed = jnp.moveaxis(outputs, 0, 1).reshape(token_rows, local_width)
    gained = (mixed * gain_mixer).astype(jnp.bfloat16)
    partial_squares = jnp.sum(mixed * mixed, axis=1)
    mixer_terms = jnp.dot(gained, w_out, preferred_element_type=jnp.float32)
    mixer_sum, squares = (
        lax.psum(mixer_terms.astype(jnp.bfloat16), "req").astype(jnp.float32),
        lax.psum(partial_squares.astype(jnp.bfloat16), "req").astype(jnp.float32),
    )
    attn = mixer_sum * lax.rsqrt(squares[:, None] / model_width + EPSILON)
    first = (residual_in.astype(jnp.float32) + attn).astype(jnp.bfloat16)
    normed = scaled_norm(first, gain_mlp)
    gate = jnp.dot(normed, w_gate, preferred_element_type=jnp.float32)
    up_part = jnp.dot(normed, w_up, preferred_element_type=jnp.float32)
    hidden = (jax.nn.silu(gate) * up_part).astype(jnp.bfloat16)
    next_weight = w_next.reshape(model_width, 3 * local_width)
    down_terms = jnp.dot(hidden, w_down, preferred_element_type=jnp.float32)
    down = lax.psum(down_terms.astype(jnp.bfloat16), "req").astype(jnp.float32)
    second = (first.astype(jnp.float32) + down).astype(jnp.bfloat16)
    final_norm = scaled_norm(second, gain_next)
    next_flat = jnp.dot(final_norm, next_weight, preferred_element_type=jnp.float32)
    next_mixer = next_flat.astype(jnp.bfloat16).reshape(token_rows, 3, local_width)
    edge_count = conv_edges.shape[1]
    edge_index = accepted[:, None] + jnp.arange(edge_count, dtype=jnp.int32)[None, :]
    kept_edge = jnp.take_along_axis(sequence, edge_index[:, :, None], axis=1)
    group_start = lax.axis_index("grp") * requests
    empty_state = jnp.zeros_like(kept_local)
    empty_edges = jnp.zeros(kept_edge.shape, jnp.float32)
    state_acc = empty_state
    edge_acc = empty_edges
    state_piece = lax.all_gather(kept_local.astype(jnp.bfloat16), "grp", axis=0, tiled=True).astype(
        jnp.float32
    )
    edge_piece = lax.all_gather(
        kept_edge.astype(jnp.float32).astype(jnp.bfloat16), "grp", axis=0, tiled=True
    ).astype(jnp.float32)
    target = home_slot - group_start
    inside = (target >= 0) & (target < requests)
    target = jnp.where(inside, target, requests)
    state_acc = state_acc.at[target].set(state_piece, mode="drop")
    edge_acc = edge_acc.at[target].set(edge_piece, mode="drop")
    return (next_mixer, state_acc, edge_acc.astype(jnp.bfloat16))


def solution(mesh):
    in_specs = (
        P("grp", None),
        P("grp", None, "req"),
        P(),
        P(None, "req"),
        P("grp", None, "req"),
        P("grp", "req", None),
        P("grp"),
        P(),
        P("req"),
        P("req", None),
        P(),
        P(None, "req"),
        P(None, "req"),
        P("req", None),
        P(),
        P(None, None, "req"),
    )
    out_specs = (P("grp", None, "req"), P("grp", "req", None), P("grp", None, "req"))
    return jax.shard_map(
        per_device, mesh=mesh, in_specs=in_specs, out_specs=out_specs, check_vma=False
    )
```

profile of v0, /device:TPU:1, one launch (start us, length us, event | category | flops | bytes accessed | tf_op | source)
XLA Modules:
  0.0 312.3 jit_solution(15410177543315030601)
XLA Ops:
  8.1 1.3 copy.83
  9.3 0.9 slice.36
  10.5 1.5 collective-permute-start
  12.0 0.8 slice.39
  12.8 0.8 slice_bitcast_fusion.3
  13.8 0.7 constant_dynamic-update-slice_fusion.1
  14.6 0.7 copy-done.4
  15.5 0.8 broadcast_subtract_fusion
  16.2 0.3 maximum_select_fusion
  16.6 0.8 subtract_bitcast_fusion
  17.4 35.0 %while.17 = (s32[]{:T(128)}, f32[32,1,64,128]{3,2,1,0:T(8,128)S(1)}, bf16[32,1,64,128]{3,2,1,0:T(8,128)(2,1)S(1)}, f32[16,32,1,64]{3,2,1,0:T(1,128)S(1)}, f32[16...) while((s32[]{:T(128)}, ...), condition=%wide.region_2.3_spmd, body=%wide.region_0.2_spmd.sunk | while | flops 1572898 | bytes 4424001 | solution.py:97
  17.4 0.9 constant_dynamic-slice_fusion.5
  18.4 0.9 multiply_reduce_fusion.3
  19.6 0.9 constant_dynamic-slice_fusion.5
  20.6 0.9 multiply_reduce_fusion.3
  21.8 0.9 constant_dynamic-slice_fusion.5
  22.8 0.9 multiply_reduce_fusion.3
  23.7 0.2 broadcast_select_fusion.3
  24.0 0.9 constant_dynamic-slice_fusion.5
  25.0 0.9 multiply_reduce_fusion.3
  25.9 0.2 broadcast_select_fusion.3
  26.2 0.9 constant_dynamic-slice_fusion.5
  27.2 0.9 multiply_reduce_fusion.3
  28.4 0.9 constant_dynamic-slice_fusion.5
  29.4 0.9 multiply_reduce_fusion.3
  30.6 0.9 constant_dynamic-slice_fusion.5
  31.5 0.9 multiply_reduce_fusion.3
  32.7 0.9 constant_dynamic-slice_fusion.5
  33.7 0.9 multiply_reduce_fusion.3
  34.9 0.9 constant_dynamic-slice_fusion.5
  35.9 0.9 multiply_reduce_fusion.3
  37.1 0.9 constant_dynamic-slice_fusion.5
  38.1 0.9 multiply_reduce_fusion.3
  39.3 0.9 constant_dynamic-slice_fusion.5
  40.3 0.9 multiply_reduce_fusion.3
  41.2 0.2 broadcast_select_fusion.3
  41.5 0.9 constant_dynamic-slice_fusion.5
  42.5 0.9 multiply_reduce_fusion.3
  43.7 0.9 constant_dynamic-slice_fusion.5
  44.7 0.9 multiply_reduce_fusion.3
  45.9 0.9 constant_dynamic-slice_fusion.5
  46.8 0.9 multiply_reduce_fusion.3
  48.0 0.9 constant_dynamic-slice_fusion.5
  49.0 0.9 multiply_reduce_fusion.3
  50.2 0.9 constant_dynamic-slice_fusion.5
  51.2 0.9 multiply_reduce_fusion.3
  52.6 2.9 convolution_convert_fusion.1
  55.6 1.1 multiply_reduce_fusion.1
  57.0 63.9 %psum.22 = bf16[512]{0:T(512)(128)(2,1)S(1)} all-reduce(bf16[512]{0:T(512)(128)(2,1)S(1)} %convert_element_type.109), channel_id=1, replica_groups=mesh['req'=32,'grp'=4] {'req'}, use_global_device_ids=true, to_apply=%region_5.6 | all-reduce | flops 512 | bytes 2048 | tf_op jit(solution)/shard_map/psum | solution.py:105
  120.9 44.4 %all-reduce.3.cloned.1.call-done = bf16[512,2048]{1,0:T(8,128)(2,1)} async-done(((bf16[512,2048]{1,0:T(8,128)(2,1)}), bf16[512,2048]{1,0:T(8,128)(2,1)}) %all-reduce.3.cloned.1.call-update) | async-done | bytes 2097168 | tf_op jit(solution)/shard_map/psum | solution.py:104
  165.3 3.2 %fusion.3 = (f32[512]{0:T(512)S(1)}, bf16[512,2048]{1,0:T(8,128)(2,1)S(1)}) fusion(f32[512]{0:T(512)S(1)} %add_rsqrt_fusion.2, bf16[512,2048]{1,0:T(8,128)(2,1)} %all-reduce.3.cloned.1.call-done, bf16[512,2048]{1,0:T(8,128)(2,1)} %param.18), kind=kLoop, calls=%fused_computation.21 | loop fusion | flops 8388096 | bytes 6295552 | tf_op jit(solution)/shard_map/reduce_sum | solution.py:21
  168.5 2.0 fusion.18
  170.6 4.3 %convolution_convert_fusion = bf16[512,2048]{1,0:T(8,128)(2,1)} fusion(bf16[176,2048]{1,0:T(8,128)(2,1)} %param.31, bf16[2048,176]{0,1:T(8,128)(2,1)} %param.30, bf16[512,2048]{1,0:T(8,128)(2,1)S(1)} %get-tuple-element.226, f32[2048]{0:T(1024)S(1)} %copy-done.8, f32[512]{0:T(512)S(1)} %add_rsqrt_fusion.1, f32[512,176]{0,1:T(8,128)S(1)} %fusion.18), kind=kOutput, calls=%fused_computation.26 | convolution fusion | flops 743981056 | bytes 6006784 | tf_op jit(solution)/shard_map/dot_general | solution.py:114
  174.9 0.5 all-gather.3.cloned.1.call-update
  175.6 1.5 gather_fusion
  177.4 9.7 %all_gather.7 = bf16[128,3,64]{2,0,1:T(8,128)(2,1)S(1)} all-gather(bf16[32,3,64]{2,0,1:T(8,128)(2,1)S(1)} %copy.53), channel_id=1, replica_groups=mesh['req'=32,'grp'=4] {'grp'}, dimensions={0}, use_global_device_ids=true | all-gather | bytes 61440 | tf_op jit(solution)/shard_map/all_gather | solution.py:131
  187.4 4.6 %scatter_fusion.1 = f32[32,3,64]{2,1,0:T(4,128)S(1)} fusion(f32[32,3,64]{2,1,0:T(4,128)S(1)} %broadcast_in_dim.72, s32[128]{0:T(128)S(1)} %compare_select_fusion.2, f32[128,3,64]{2,1,0:T(4,128)S(1)} %copy.55), kind=kCustom, calls=%fused_computation.2 | custom fusion | bytes 295424 | tf_op jit(solution)/shard_map/scatter | solution.py:138
  192.0 0.6 copy.56
  192.7 90.1 %all-reduce.5.cloned.1.call-done = bf16[512,2048]{1,0:T(8,128)(2,1)} async-done(((bf16[512,2048]{1,0:T(8,128)(2,1)}), bf16[512,2048]{1,0:T(8,128)(2,1)}) %all-reduce.5.cloned.1.call-update) | async-done | bytes 2097168 | tf_op jit(solution)/shard_map/psum | solution.py:115
  282.7 2.5 fusion
  285.3 1.8 fusion.11
  287.0 4.0 %bitcast_convert_fusion = f32[128,64,128]{2,1,0:T(8,128)} fusion(bf16[128,1,64,128]{3,2,1,0:T(8,128)(2,1)} %all-gather.3.cloned.1.call-done), kind=kLoop, calls=%fused_computation.29 | loop fusion | flops 1048576 | bytes 6291456 | tf_op jit(solution)/shard_map/convert_element_type | solution.py:128
  291.1 12.8 %scatter_fusion = f32[32,64,128]{2,1,0:T(8,128)S(1)} fusion(f32[32,64,128]{2,1,0:T(8,128)S(1)} %broadcast_in_dim.70, s32[128]{0:T(128)S(1)} %compare_select_fusion.2, f32[128,64,128]{2,1,0:T(8,128)} %bitcast_convert_fusion), kind=kCustom, calls=%fused_computation.1 | custom fusion | bytes 12583424 | tf_op jit(solution)/shard_map/scatter | solution.py:137
  303.9 1.0 copy-done.1
  (149 shorter events, 5.8 us)
Async XLA Ops:
  8.0 277.2 %copy-start = (bf16[2048,3,64]{0,2,1:T(8,128)(2,1)S(1)}, bf16[2048,3,64]{0,2,1:T(8,128)(2,1)}, u32[]{:S(2)}) copy-start(bf16[2048,3,64]{0,2,1:T(8,128)(2,1)} %param.33) | copy-start | bytes 2359300
  8.0 157.3 %all-reduce.3.cloned.1.call-start = ((), (), s32[]{:S(2)}) async-start(), calls=%async_computation | async-start | bytes 4194304 | tf_op jit(solution)/shard_map/psum | solution.py:104
  9.3 8.1 %copy-start.7 = (s32[32]{0:T(128)S(1)}, s32[32]{0:T(128)}, u32[]{:S(2)}) copy-start(s32[32]{0:T(128)} %param.24) | copy-start | bytes 388
  10.5 5.8 %collective-permute-start = (bf16[512,2,64]{2,0,1:T(8,128)(2,1)S(1)}, bf16[512,2,64]{2,0,1:T(8,128)(2,1)S(1)}, u32[]{:S(2)}, u32[]{:S(2)}) collective-permute-start(bf16[512,2,64]{2,0,1:T(8,128)(2,1)S(1)} %copy.60), channel_id=1, source_target_pairs={{0,4},{4,0},{8,12},{12,8},{16,20},{20,16},{24,28},{28,24},{32,36},... | collective-permute-start | bytes 393224 | tf_op jit(solution)/shard_map/ppermute | solution.py:16
  14.5 0.7 copy-start.4
  17.4 35.1 %copy-start.6 = (f32[64]{0:T(128)S(1)}, f32[64]{0:T(128)}, u32[]{:S(2)}) copy-start(f32[64]{0:T(128)} %param.26) | copy-start | bytes 772
  52.4 116.1 %copy-start.2 = (bf16[32,1,64,128]{3,2,1,0:T(8,128)(2,1)}, bf16[32,1,64,128]{3,2,1,0:T(8,128)(2,1)S(1)}, u32[]{:S(2)}) copy-start(bf16[32,1,64,128]{3,2,1,0:T(8,128)(2,1)S(1)} %get-tuple-element.159) | copy-start | bytes 1572868
  55.6 113.0 %copy-start.8 = (f32[2048]{0:T(1024)S(1)}, f32[2048]{0:T(1024)}, u32[]{:S(2)}) copy-start(f32[2048]{0:T(1024)} %param.28) | copy-start | bytes 24580
  55.6 227.1 %all-reduce.5.cloned.1.call-start = ((), (), s32[]{:S(2)}) async-start(), calls=%async_computation.1 | async-start | bytes 4194304 | tf_op jit(solution)/shard_map/psum | solution.py:115
  170.6 5.1 %copy-start.5 = (bf16[32,19,64]{2,0,1:T(8,128)(2,1)S(1)}, bf16[32,19,64]{2,0,1:T(8,128)(2,1)}, u32[]{:S(2)}) copy-start(bf16[32,19,64]{2,0,1:T(8,128)(2,1)} %copy-done.4) | copy-start | bytes 233476
  170.6 16.8 %copy-start.10 = (s32[128]{0:T(128)S(1)}, s32[128]{0:T(128)}, u32[]{:S(2)}) copy-start(s32[128]{0:T(128)} %param.25) | copy-start | bytes 1540
  174.8 110.4 %copy-start.9 = (f32[2048]{0:T(1024)S(1)}, f32[2048]{0:T(1024)}, u32[]{:S(2)}) copy-start(f32[2048]{0:T(1024)} %param.32) | copy-start | bytes 24580
  174.9 112.2 %all-gather.3.cloned.1.call-start = ((), (), s32[]{:S(2)}) async-start(), calls=%async_computation.2 | async-start | bytes 2621440 | tf_op jit(solution)/shard_map/all_gather | solution.py:128
  282.7 2.5 copy-start.3
  303.9 1.0 copy-start.1
Sparse Core Ops, SparseCore 0:
  55.7 109.5 all-reduce.2
  175.0 107.6 all-reduce.4
Sparse Core Ops, SparseCore 1:
  177.6 30.1 all-gather.2
where the time goes:
time: 313 us; the launch traced here: 312 us
  waiting for transfers between devices  135 us (43%)
  blocking collectives  73.7 us (24%)
  local copies, waits for them, and re-layouts  42.7 us (14%)
  other arithmetic  31.4 us (10%)
  between operations  15.9 us (5%)
  matrix products  11 us (4%)
    psum x1, waiting for transfers between devices, per_device(): down = lax.psum(down_terms.astype(jnp.bfloat16), 'req').astype(jnp.float32)  90.1 us
    psum x1, blocking collectives, per_device(): lax.psum(partial_squares.astype(jnp.bfloat16), 'req').astype(jnp.float32)  63.9 us
    psum x1, waiting for transfers between devices, per_device(): lax.psum(mixer_terms.astype(jnp.bfloat16), 'req').astype(jnp.float32)  44.4 us
    dynamic_slice x32, local copies, waits for them, and re-layouts, per_device(): lax.scan(advance, (begin_state, begin_state, jnp.int32(0)), step_inputs)  15.3 us
    reduce_sum x16, other arithmetic, advance(): output = jnp.sum(current * q_step[:, :, None, :], axis=3) * head_scale  14.5 us
    scatter x1, local copies, waits for them, and re-layouts, per_device(): state_acc = state_acc.at[target].set(state_piece, mode='drop')  12.8 us
    all_gather x1, blocking collectives, per_device(): lax.all_gather(kept_edge.astype(jnp.float32).astype(jnp.bfloat16), 'grp',...  9.73 us
  transfers between devices with their start and end apart: 4, of which 2 were waited for; matrix products, arithmetic and copies ran while one was open for 5% of the time, Pallas kernels for 0%

commit v1 on v0

--- a/solution.py
+++ b/solution.py
@@ -4,6 +4,13 @@
 from jax.sharding import PartitionSpec as P
 
 EPSILON = 1e-06
+
+
+def pack_digits(point, mesh_name):
+    top = jnp.concatenate(
+        lax.all_to_all(jnp.stack(lax.axis_size(mesh_name) * [point]), mesh_name, 0, 0), axis=0
+    )
+    return top
 
 
 def partner_2(block, axis, apart):
@@ -128,8 +135,8 @@
     state_piece = lax.all_gather(kept_local.astype(jnp.bfloat16), "grp", axis=0, tiled=True).astype(
         jnp.float32
     )
-    edge_piece = lax.all_gather(
-        kept_edge.astype(jnp.float32).astype(jnp.bfloat16), "grp", axis=0, tiled=True
+    edge_piece = pack_digits(
+        kept_edge.astype(jnp.float32).astype(jnp.bfloat16), mesh_name="grp"
     ).astype(jnp.float32)
     target = home_slot - group_start
     inside = (target >= 0) & (target < requests)

time: 313 us -> 314 us (level)
  blocking collectives: 73.7 us -> 63.9 us
  waiting for transfers between devices: 135 us -> 140 us
  starting transfers between devices: 1.62 us -> 5.59 us
    all_gather x1 -> x0, blocking collectives: 9.73 us -> none  [per_device(): lax.all_gather(kept_edge.astype(jnp.float32).astype(jnp.bfloat16), 'grp',...]
    all_to_all x0 -> x1, waiting for transfers between devices: none -> 4.38 us  [pack_digits(): lax.all_to_all(jnp.stack(lax.axis_size(mesh_name) * [point]), mesh_name,...]
    all_to_all x0 -> x1, starting transfers between devices: none -> 3.97 us  [pack_digits(): lax.all_to_all(jnp.stack(lax.axis_size(mesh_name) * [point]), mesh_name,...]
  transfers between devices with their start and end apart: 4 -> 5, of which waited for: 2 -> 3; matrix products, arithmetic and copies ran while one was open for 5% -> 6% of each run, Pallas kernels for 0% -> 0%
where the time goes in v1:
time: 314 us; the launch traced here: 312 us
  waiting for transfers between devices  140 us (45%)
  blocking collectives  63.9 us (20%)
  local copies, waits for them, and re-layouts  43.5 us (14%)
  other arithmetic  31.4 us (10%)
  between operations  15.9 us (5%)
  matrix products  11 us (4%)
  starting transfers between devices  5.59 us (2%)
    psum x1, waiting for transfers between devices, per_device(): down = lax.psum(down_terms.astype(jnp.bfloat16), 'req').astype(jnp.float32)  90.7 us
    psum x1, blocking collectives, per_device(): lax.psum(partial_squares.astype(jnp.bfloat16), 'req').astype(jnp.float32)  63.9 us
    psum x1, waiting for transfers between devices, per_device(): lax.psum(mixer_terms.astype(jnp.bfloat16), 'req').astype(jnp.float32)  44.4 us
    dynamic_slice x32, local copies, waits for them, and re-layouts, per_device(): lax.scan(advance, (begin_state, begin_state, jnp.int32(0)), step_inputs)  15.3 us
    reduce_sum x16, other arithmetic, advance(): output = jnp.sum(current * q_step[:, :, None, :], axis=3) * head_scale  14.5 us
    scatter x1, local copies, waits for them, and re-layouts, per_device(): state_acc = state_acc.at[target].set(state_piece, mode='drop')  12.8 us
  transfers between devices with their start and end apart: 5, of which 3 were waited for; matrix products, arithmetic and copies ran while one was open for 6% of the time, Pallas kernels for 0%

profile of v1, /device:TPU:1, one launch (start us, length us, event | category | flops | bytes accessed | tf_op | source)
XLA Modules:
  0.0 312.4 jit_solution(725874935502439801)
XLA Ops:
  8.1 1.3 copy.95
  9.3 0.9 slice.36
  10.5 1.5 collective-permute-start
  12.0 0.8 slice.39
  12.8 0.8 slice_bitcast_fusion.3
  13.8 0.7 constant_dynamic-update-slice_fusion.1
  14.6 0.7 copy-done.4
  15.5 0.8 broadcast_subtract_fusion
  16.2 0.3 maximum_select_fusion
  16.6 0.8 subtract_bitcast_fusion
  17.4 35.0 %while.17 = (s32[]{:T(128)}, f32[32,1,64,128]{3,2,1,0:T(8,128)S(1)}, bf16[32,1,64,128]{3,2,1,0:T(8,128)(2,1)S(1)}, f32[16,32,1,64]{3,2,1,0:T(1,128)S(1)}, f32[16...) while((s32[]{:T(128)}, ...), condition=%wide.region_2.3_spmd, body=%wide.region_0.2_spmd.sunk | while | flops 1572898 | bytes 4424001 | solution.py:104
  17.4 0.9 constant_dynamic-slice_fusion.5
  18.4 0.9 multiply_reduce_fusion.3
  19.6 0.9 constant_dynamic-slice_fusion.5
  20.6 0.9 multiply_reduce_fusion.3
  21.8 0.9 constant_dynamic-slice_fusion.5
  22.8 0.9 multiply_reduce_fusion.3
  23.7 0.2 broadcast_select_fusion.3
  24.0 0.9 constant_dynamic-slice_fusion.5
  25.0 0.9 multiply_reduce_fusion.3
  26.2 0.9 constant_dynamic-slice_fusion.5
  27.2 0.9 multiply_reduce_fusion.3
  28.4 0.9 constant_dynamic-slice_fusion.5
  29.4 0.9 multiply_reduce_fusion.3
  30.6 0.9 constant_dynamic-slice_fusion.5
  31.5 0.9 multiply_reduce_fusion.3
  32.7 0.9 constant_dynamic-slice_fusion.5
  33.7 0.9 multiply_reduce_fusion.3
  34.9 0.9 constant_dynamic-slice_fusion.5
  35.9 0.9 multiply_reduce_fusion.3
  37.1 0.9 constant_dynamic-slice_fusion.5
  38.1 0.9 multiply_reduce_fusion.3
  39.3 0.9 constant_dynamic-slice_fusion.5
  40.3 0.9 multiply_reduce_fusion.3
  41.5 0.9 constant_dynamic-slice_fusion.5
  42.5 0.9 multiply_reduce_fusion.3
  43.7 0.9 constant_dynamic-slice_fusion.5
  44.7 0.9 multiply_reduce_fusion.3
  45.9 0.9 constant_dynamic-slice_fusion.5
  46.8 0.9 multiply_reduce_fusion.3
  48.0 0.9 constant_dynamic-slice_fusion.5
  49.0 0.9 multiply_reduce_fusion.3
  50.2 0.9 constant_dynamic-slice_fusion.5
  51.2 0.9 multiply_reduce_fusion.3
  52.6 2.9 convolution_convert_fusion.1
  55.6 1.1 multiply_reduce_fusion.1
  56.9 63.9 %psum.22 = bf16[512]{0:T(512)(128)(2,1)S(1)} all-reduce(bf16[512]{0:T(512)(128)(2,1)S(1)} %convert_element_type.112), channel_id=1, replica_groups=mesh['req'=32,'grp'=4] {'req'}, use_global_device_ids=true, to_apply=%region_5.6 | all-reduce | flops 512 | bytes 2048 | tf_op jit(solution)/shard_map/psum | solution.py:112
  120.9 44.4 %all-reduce.3.cloned.1.call-done = bf16[512,2048]{1,0:T(8,128)(2,1)} async-done(((bf16[512,2048]{1,0:T(8,128)(2,1)}), bf16[512,2048]{1,0:T(8,128)(2,1)}) %all-reduce.3.cloned.1.call-update) | async-done | bytes 2097168 | tf_op jit(solution)/shard_map/psum | solution.py:111
  165.3 3.2 %fusion.3 = (f32[512]{0:T(512)S(1)}, bf16[512,2048]{1,0:T(8,128)(2,1)S(1)}) fusion(f32[512]{0:T(512)S(1)} %add_rsqrt_fusion.2, bf16[512,2048]{1,0:T(8,128)(2,1)} %all-reduce.3.cloned.1.call-done, bf16[512,2048]{1,0:T(8,128)(2,1)} %param.18), kind=kLoop, calls=%fused_computation.21 | loop fusion | flops 8388096 | bytes 6295552 | tf_op jit(solution)/shard_map/reduce_sum | solution.py:28
  168.5 2.0 fusion.18
  170.6 4.2 %convolution_convert_fusion = bf16[512,2048]{1,0:T(8,128)(2,1)} fusion(bf16[176,2048]{1,0:T(8,128)(2,1)} %param.31, bf16[2048,176]{0,1:T(8,128)(2,1)} %param.30, bf16[512,2048]{1,0:T(8,128)(2,1)S(1)} %get-tuple-element.238, f32[2048]{0:T(1024)S(1)} %copy-done.8, f32[512]{0:T(512)S(1)} %add_rsqrt_fusion.1, f32[512,176]{0,1:T(8,128)S(1)} %fusion.18), kind=kOutput, calls=%fused_computation.26 | convolution fusion | flops 743981056 | bytes 6006784 | tf_op jit(solution)/shard_map/dot_general | solution.py:121
  174.9 0.5 all-gather.3.cloned.1.call-update
  175.6 1.5 gather_fusion
  177.4 0.7 reshape.293
  178.2 4.0 %all-to-all-start = ((bf16[4,2,3072]{2,1,0:T(2,128)(2,1)}), bf16[4,2,3072]{2,1,0:T(2,128)(2,1)S(1)}, u32[]{:S(2)}, u32[]{:S(2)}) async-start(bf16[4,2,3072]{2,1,0:T(2,128)(2,1)} %reshape.293), calls=%async_computation | async-start | bytes 98304 | tf_op jit(solution)/shard_map/all_to_all | solution.py:11
  182.1 4.4 %all-to-all-done = bf16[4,2,3072]{2,1,0:T(2,128)(2,1)S(1)} async-done(((bf16[4,2,3072]{2,1,0:T(2,128)(2,1)}), bf16[4,2,3072]{2,1,0:T(2,128)(2,1)S(1)}, u32[]{:S(2)}, u32[]{:S(2)}) %all-to-all-start) | async-done | bytes 49184 | tf_op jit(solution)/shard_map/all_to_all | solution.py:11
  186.8 4.6 %scatter_fusion.1 = f32[32,3,64]{2,1,0:T(4,128)S(1)} fusion(f32[32,3,64]{2,1,0:T(4,128)S(1)} %broadcast_in_dim.72, s32[128]{0:T(128)S(1)} %compare_select_fusion.2, f32[128,3,64]{2,1,0:T(4,128)S(1)} %copy.67), kind=kCustom, calls=%fused_computation.2 | custom fusion | bytes 295424 | tf_op jit(solution)/shard_map/scatter | solution.py:145
  191.4 0.6 copy.68
  192.1 90.7 %all-reduce.5.cloned.1.call-done = bf16[512,2048]{1,0:T(8,128)(2,1)} async-done(((bf16[512,2048]{1,0:T(8,128)(2,1)}), bf16[512,2048]{1,0:T(8,128)(2,1)}) %all-reduce.5.cloned.1.call-update) | async-done | bytes 2097168 | tf_op jit(solution)/shard_map/psum | solution.py:122
  282.8 2.5 fusion
  285.3 1.8 fusion.11
  287.1 4.0 %bitcast_convert_fusion = f32[128,64,128]{2,1,0:T(8,128)} fusion(bf16[128,1,64,128]{3,2,1,0:T(8,128)(2,1)} %all-gather.3.cloned.1.call-done), kind=kLoop, calls=%fused_computation.29 | loop fusion | flops 1048576 | bytes 6291456 | tf_op jit(solution)/shard_map/convert_element_type | solution.py:135
  291.2 12.8 %scatter_fusion = f32[32,64,128]{2,1,0:T(8,128)S(1)} fusion(f32[32,64,128]{2,1,0:T(8,128)S(1)} %broadcast_in_dim.70, s32[128]{0:T(128)S(1)} %compare_select_fusion.2, f32[128,64,128]{2,1,0:T(8,128)} %bitcast_convert_fusion), kind=kCustom, calls=%fused_computation.1 | custom fusion | bytes 12583424 | tf_op jit(solution)/shard_map/scatter | solution.py:144
  304.0 1.0 copy-done.1
  (153 shorter events, 6.3 us)
Async XLA Ops:
  8.0 277.3 %copy-start = (bf16[2048,3,64]{0,2,1:T(8,128)(2,1)S(1)}, bf16[2048,3,64]{0,2,1:T(8,128)(2,1)}, u32[]{:S(2)}) copy-start(bf16[2048,3,64]{0,2,1:T(8,128)(2,1)} %param.33) | copy-start | bytes 2359300
  8.0 157.2 %all-reduce.3.cloned.1.call-start = ((), (), s32[]{:S(2)}) async-start(), calls=%async_computation.1 | async-start | bytes 4194304 | tf_op jit(solution)/shard_map/psum | solution.py:111
  9.3 8.1 %copy-start.7 = (s32[32]{0:T(128)S(1)}, s32[32]{0:T(128)}, u32[]{:S(2)}) copy-start(s32[32]{0:T(128)} %param.24) | copy-start | bytes 388
  10.5 5.8 %collective-permute-start = (bf16[512,2,64]{2,0,1:T(8,128)(2,1)S(1)}, bf16[512,2,64]{2,0,1:T(8,128)(2,1)S(1)}, u32[]{:S(2)}, u32[]{:S(2)}) collective-permute-start(bf16[512,2,64]{2,0,1:T(8,128)(2,1)S(1)} %copy.72), channel_id=1, source_target_pairs={{0,4},{4,0},{8,12},{12,8},{16,20},{20,16},{24,28},{28,24},{32,36},... | collective-permute-start | bytes 393224 | tf_op jit(solution)/shard_map/ppermute | solution.py:23
  14.5 0.7 copy-start.4
  17.4 35.1 %copy-start.6 = (f32[64]{0:T(128)S(1)}, f32[64]{0:T(128)}, u32[]{:S(2)}) copy-start(f32[64]{0:T(128)} %param.26) | copy-start | bytes 772
  52.4 116.1 %copy-start.2 = (bf16[32,1,64,128]{3,2,1,0:T(8,128)(2,1)}, bf16[32,1,64,128]{3,2,1,0:T(8,128)(2,1)S(1)}, u32[]{:S(2)}) copy-start(bf16[32,1,64,128]{3,2,1,0:T(8,128)(2,1)S(1)} %get-tuple-element.159) | copy-start | bytes 1572868
  55.6 113.0 %copy-start.8 = (f32[2048]{0:T(1024)S(1)}, f32[2048]{0:T(1024)}, u32[]{:S(2)}) copy-start(f32[2048]{0:T(1024)} %param.28) | copy-start | bytes 24580
  55.6 227.2 %all-reduce.5.cloned.1.call-start = ((), (), s32[]{:S(2)}) async-start(), calls=%async_computation.2 | async-start | bytes 4194304 | tf_op jit(solution)/shard_map/psum | solution.py:122
  170.6 5.1 %copy-start.5 = (bf16[32,19,64]{2,0,1:T(8,128)(2,1)S(1)}, bf16[32,19,64]{2,0,1:T(8,128)(2,1)}, u32[]{:S(2)}) copy-start(bf16[32,19,64]{2,0,1:T(8,128)(2,1)} %copy-done.4) | copy-start | bytes 233476
  170.6 11.6 %copy-start.10 = (s32[128]{0:T(128)S(1)}, s32[128]{0:T(128)}, u32[]{:S(2)}) copy-start(s32[128]{0:T(128)} %param.25) | copy-start | bytes 1540
  174.8 110.4 %copy-start.9 = (f32[2048]{0:T(1024)S(1)}, f32[2048]{0:T(1024)}, u32[]{:S(2)}) copy-start(f32[2048]{0:T(1024)} %param.32) | copy-start | bytes 24580
  174.9 112.2 %all-gather.3.cloned.1.call-start = ((), (), s32[]{:S(2)}) async-start(), calls=%async_computation.3 | async-start | bytes 2621440 | tf_op jit(solution)/shard_map/all_gather | solution.py:135
  178.2 8.4 %all-to-all-start = ((bf16[4,2,3072]{2,1,0:T(2,128)(2,1)}), bf16[4,2,3072]{2,1,0:T(2,128)(2,1)S(1)}, u32[]{:S(2)}, u32[]{:S(2)}) async-start(bf16[4,2,3072]{2,1,0:T(2,128)(2,1)} %reshape.293), calls=%async_computation | async-start | bytes 98304 | tf_op jit(solution)/shard_map/all_to_all | solution.py:11
  282.8 2.5 copy-start.3
  304.0 1.0 copy-start.1
Sparse Core Ops, SparseCore 0:
  55.7 109.5 all-reduce.2
  175.0 107.7 all-reduce.4
Sparse Core Ops, SparseCore 1:
  177.6 30.0 all-gather.2
